TPU v7x, 32 devices: a whole 2x2x4 slice. The times are simulated.
32 devices in a mesh: groups: 2 (over y), mp: 4 (over z), example: 4 (over x, core).
Axes of the slice: x: 2, y: 2, z: 4, core: 2. Of those that a mesh axis runs over, the one named last changes fastest.
Arguments:
- inputs: bfloat16 [2, 24576, 28672], P(None, ('groups', 'example'), 'mp'), parts along dimension 1, may hold values from -6 to 6
- out_grads: bfloat16 [2, 24576, 8192], P(None, ('groups', 'example', 'mp')), parts along dimension 1, may hold values from -6 to 6
- lengths: int32 [24], P(('groups', 'example')), parts along dimension 0, may hold values from 128 to 1024, as said below
- proj_in: bfloat16 [2, 28672, 64], P(None, 'mp'), may hold values from -0.03125 to 0.03125
- proj_out: bfloat16 [2, 8192, 64], replicated, may hold values from -0.0625 to 0.0625
- queries: bfloat16 [1024, 8192], P('example', 'mp'), may hold values from -0.0029296875 to 0.0029296875
Outputs:
- logged: bfloat16 [24, 8192], P(('groups', 'example'), 'mp'), parts along dimension 0
- scores: float32 [24, 1024], P(('groups', 'example')), parts along dimension 0
There are 2 independent parts, one for each index of `groups`. A program takes and returns all parts, laid end to end along the dimension named above; an argument that names none is the same for every part. Nothing has to cross between parts.
Inputs may be any that keep to these rules, and one draw needn't show every extreme that they name: `lengths`: slots at or past an example's length are padding; in every draw some example is full (1024).
All inputs are finite; a program needn't handle non-finite values.
Results may differ from a plain program's by a relative error of at most 0.005.
Values may be sent and summed in bfloat16 or wider, within the bound.
No kernel may reach another device: no remote copies, remote signals or barrier semaphores. Data moves between devices by JAX's collectives and lax.ppermute only.
A program may use at most 256 MiB of HBM per device.

v0:
```python
import jax
import jax.numpy as jnp
from jax import lax
from jax.sharding import PartitionSpec as P


def outer_grads(left_rows, right_rows, ex_dev, seq_len, layers, proj_rank):
    left_wide = left_rows.astype(jnp.float32).reshape(ex_dev, seq_len, layers, proj_rank)
    right_wide = right_rows.reshape(ex_dev, seq_len, layers, proj_rank)
    return jnp.einsum("esli,eslj->elij", left_wide, right_wide, precision=lax.Precision.HIGH)


def on_device(inputs, out_grads, lengths, proj_in, proj_out, queries):
    layers = inputs.shape[0]
    tok_dev = inputs.shape[1]
    ex_dev = lengths.shape[0]
    seq_len = tok_dev // ex_dev
    proj_rank = proj_in.shape[2]
    shard_count = lax.axis_size("mp")
    tok_mp = tok_dev // shard_count
    row_base = lax.axis_index("mp") * tok_mp
    row_ids = row_base + jnp.arange(tok_mp, dtype=jnp.int32)
    owners = row_ids // seq_len
    within = row_ids % seq_len
    limits = jnp.sum(
        jnp.where(
            owners[:, None] == jnp.arange(ex_dev, dtype=jnp.int32)[None, :], lengths[None, :], 0
        ),
        axis=1,
    )
    is_live = within < limits
    projected = jnp.concatenate(
        [
            jnp.dot(out_grads[layer_idx], proj_out[layer_idx], preferred_element_type=jnp.float32)
            for layer_idx in range(layers)
        ],
        axis=1,
    )
    outer_side = jnp.where(is_live[:, None], projected, jnp.float32(0.0)).astype(jnp.bfloat16)
    outer_side = lax.optimization_barrier(outer_side)
    pieces = [
        jnp.dot(inputs[layer_idx], proj_in[layer_idx], preferred_element_type=jnp.float32)
        for layer_idx in range(layers)
    ]
    local_side = jnp.concatenate(pieces, axis=1)
    gathered = lax.all_gather(outer_side, "mp", axis=0, tiled=True)
    grads = outer_grads(gathered, local_side, ex_dev, seq_len, layers, proj_rank)
    flat_grads = grads.reshape(ex_dev, layers * proj_rank * proj_rank)
    my_share = lax.psum_scatter(flat_grads, "mp", scatter_dimension=1, tiled=True)
    logged = my_share.astype(jnp.bfloat16)
    everyone = lax.all_gather(logged, "example", axis=0, tiled=True)
    score_part = lax.dot_general(
        everyone, queries, (((1,), (1,)), ((), ())), preferred_element_type=jnp.float32
    )
    partial_scores = lax.all_to_all(score_part, "example", split_axis=0, concat_axis=1, tiled=True)
    scores = lax.psum(partial_scores, "mp")
    return (logged, scores)


def solution(mesh):
    placed = (
        P(None, ("groups", "example"), "mp"),
        P(None, ("groups", "example", "mp"), None),
        P(("groups", "example")),
        P(None, "mp", None),
        P(),
        P("example", "mp"),
    )
    return jax.shard_map(
        on_device,
        mesh=mesh,
        in_specs=placed,
        out_specs=(P(("groups", "example"), "mp"), P(("groups", "example"), None)),
        check_vma=False,
    )
```

profile of v0, /device:TPU:0, one launch (start us, length us, event | category | flops | bytes accessed | tf_op | source)
XLA Modules:
  0.0 212.9 jit_solution(915750122538916613)
XLA Ops:
  7.2 0.0 copy-start
  7.2 0.0 reduce-scatter.4.cloned.1.call-start
  7.2 0.0 copy-start.3
  7.2 8.9 %fusion.6 = bf16[768,64]{0,1:T(8,128)(2,1)S(1)} fusion(bf16[2,768,8192]{2,1,0:T(8,128)(2,1)} %param.7, bf16[2,8192,64]{1,2,0:T(8,128)(2,1)} %param.10), kind=kOutput, calls=%fused_computation.6 | convolution fusion | flops 805306368 | bytes 13729792 | tf_op jit(solution)/shard_map/dot_general | solution.py:34
  16.1 0.0 copy-done.3
  16.1 0.0 copy-start.4
  16.1 8.6 %fusion.8 = bf16[768,64]{0,1:T(8,128)(2,1)S(1)} fusion(bf16[2,768,8192]{2,1,0:T(8,128)(2,1)} %param.7, bf16[2,8192,64]{1,2,0:T(8,128)(2,1)S(1)} %copy-done.3), kind=kOutput, calls=%fused_computation.8 | convolution fusion | flops 805306368 | bytes 13729792 | tf_op jit(solution)/shard_map/dot_general | solution.py:34
  24.8 0.0 copy-done.4
  24.8 19.7 %fusion = f32[3072,64]{0,1:T(8,128)S(1)} fusion(bf16[2,3072,7168]{2,1,0:T(8,128)(2,1)} %param.6, bf16[2,7168,64]{1,2,0:T(8,128)(2,1)S(1)} %copy-done.4), kind=kOutput, calls=%fused_computation | convolution fusion | flops 2818572288 | bytes 45744128 | tf_op jit(solution)/shard_map/dot_general | solution.py:42
  44.4 0.0 copy-start.2
  44.5 19.5 %fusion.2 = f32[3072,64]{0,1:T(8,128)S(1)} fusion(bf16[2,3072,7168]{2,1,0:T(8,128)(2,1)} %param.6, bf16[2,7168,64]{1,2,0:T(8,128)(2,1)S(1)} %copy-done.4), kind=kOutput, calls=%fused_computation.2 | convolution fusion | flops 2818572288 | bytes 45744128 | tf_op jit(solution)/shard_map/dot_general | solution.py:42
  64.0 0.0 copy-done.2
  64.0 0.1 select_reduce_fusion
  64.1 21.3 %all_gather.6 = bf16[3072,128]{0,1:T(8,128)(2,1)S(1)} all-gather(bf16[768,128]{0,1:T(8,128)(2,1)S(1)} %fusion.23), channel_id=1, replica_groups=mesh['groups'=2,'mp'=4,'example'=4] {'mp'}, dimensions={0}, use_global_device_ids=true | all-gather | bytes 983040 | tf_op jit(solution)/shard_map/all_gather | solution.py:46
  85.4 1.9 reshape.52
  87.4 1.3 pad_maximum_fusion
  88.6 2.8 %reshape.53 = f32[3,1024,2,64]{1,0,3,2:T(4,128)S(1)} reshape(f32[3072,128]{0,1:T(8,128)} %pad_maximum_fusion) | data formatting | bytes 3145728 | tf_op jit(solution)/shard_map/reshape | solution.py:9
  91.5 3.1 %fusion.12 = f32[3,2,64,64]{3,2,1,0:T(8,128)S(1)} fusion(f32[3,1024,2,64]{1,0,3,2:T(4,128)S(1)} %reshape.53, bf16[3,1024,2,64]{1,0,3,2:T(4,128)(2,1)} %reshape.52), kind=kOutput, calls=%fused_computation.13 | convolution fusion | flops 150994944 | bytes 2457600 | tf_op jit(solution)/shard_map/esli,eslj->elij/dot_general | solution.py:10
  94.6 2.7 %copy.19 = f32[3,2,64,64]{0,3,2,1:T(8,128)} copy(f32[3,2,64,64]{3,2,1,0:T(8,128)S(1)} %fusion.12) | data formatting | bytes 196608
  97.3 0.0 reduce-scatter.4.cloned.1.call-update
  97.3 76.3 %reduce-scatter.4.cloned.1.call-done = f32[2048,3]{1,0:T(8,128)} async-done(((f32[8192,3]{1,0:T(8,128)}), f32[2048,3]{1,0:T(8,128)}) %reduce-scatter.4.cloned.1.call-update) | async-done | bytes 24592
  173.6 1.6 copy.18
  175.2 0.0 copy-start.1
  175.2 5.2 %all-gather = bf16[4,3,2048]{2,1,0:T(4,128)(2,1)S(1)} all-gather(bf16[1,3,2048]{2,1,0:T(4,128)(2,1)S(1)} %bitcast.40), channel_id=1, replica_groups=mesh['groups'=2,'mp'=4,'example'=4] {'example'}, dimensions={0}, use_global_device_ids=true | all-gather | bytes 61440 | tf_op jit(solution)/shard_map/all_gather | solution.py:51
  180.5 0.0 copy-done
  180.5 0.4 fusion.30
  180.9 6.4 %all_to_all.19 = f32[4,3,256]{2,1,0:T(4,128)S(1)} all-to-all(f32[4,3,256]{2,1,0:T(4,128)S(1)} %all_to_all.14), channel_id=1, replica_groups=mesh['groups'=2,'mp'=4,'example'=4] {'example'}, dimensions={0} | all-to-all | bytes 24576 | tf_op jit(solution)/shard_map/all_to_all | solution.py:55
  187.3 18.8 %psum.7 = f32[3,1024]{1,0:T(4,128)} all-reduce(f32[3,1024]{1,0:T(4,128)S(1)} %bitcast.41), channel_id=1, replica_groups=mesh['groups'=2,'mp'=4,'example'=4] {'mp'}, use_global_device_ids=true, to_apply=%region_2.3 | all-reduce | flops 3072 | bytes 24576 | tf_op jit(solution)/shard_map/psum | solution.py:56
  206.1 0.0 copy-done.1
  (5 shorter events, 0.1 us)
Async XLA Ops:
  7.2 173.3 %copy-start = (bf16[256,2048]{1,0:T(8,128)(2,1)S(1)}, bf16[256,2048]{1,0:T(8,128)(2,1)}, u32[]{:S(2)}) copy-start(bf16[256,2048]{1,0:T(8,128)(2,1)} %param.11) | copy-start | bytes 3145732
  7.2 166.4 %reduce-scatter.4.cloned.1.call-start = ((), (), s32[]{:S(2)}) async-start(), calls=%async_computation.2 | async-start | bytes 5242880
  7.2 8.9 %copy-start.3 = (bf16[2,8192,64]{1,2,0:T(8,128)(2,1)S(1)}, bf16[2,8192,64]{1,2,0:T(8,128)(2,1)}, u32[]{:S(2)}) copy-start(bf16[2,8192,64]{1,2,0:T(8,128)(2,1)} %param.10) | copy-start | bytes 6291460
  16.1 8.6 %copy-start.4 = (bf16[2,7168,64]{1,2,0:T(8,128)(2,1)S(1)}, bf16[2,7168,64]{1,2,0:T(8,128)(2,1)}, u32[]{:S(2)}) copy-start(bf16[2,7168,64]{1,2,0:T(8,128)(2,1)} %param.9) | copy-start | bytes 5505028
  44.4 19.5 %copy-start.2 = (s32[3]{0:T(128)S(1)}, s32[3]{0:T(128)}, u32[]{:S(2)}) copy-start(s32[3]{0:T(128)} %param.8) | copy-start | bytes 40
  175.2 30.9 %copy-start.1 = (bf16[3,2048]{1,0:T(4,128)(2,1)}, bf16[3,2048]{1,0:T(4,128)(2,1)S(1)}, u32[]{:S(2)}) copy-start(bf16[3,2048]{1,0:T(4,128)(2,1)S(1)} %copy.18) | copy-start | bytes 36868
Sparse Core Ops, SparseCore 0:
  97.5 76.1 reduce-scatter.3
where the time goes:
time: 213 us
  waiting for transfers between devices  76.3 us (36%)
  matrix products  60.1 us (28%)
  blocking collectives  51.7 us (24%)
  between operations  14.2 us (7%)
  local copies, waits for them, and re-layouts  9.14 us (4%)
    unnamed x2, waiting for transfers between devices  76.3 us
    dot_general x2, matrix products, on_device(): jnp.dot(inputs[layer_idx], proj_in[layer_idx], preferred_element_type=jnp...  39.1 us
    all_gather x1, blocking collectives, on_device(): gathered = lax.all_gather(outer_side, 'mp', axis=0, tiled=True)  21.3 us
    psum x1, blocking collectives, on_device(): scores = lax.psum(partial_scores, 'mp')  18.8 us
    dot_general x2, matrix products, on_device(): jnp.dot(out_grads[layer_idx], proj_out[layer_idx], preferred_element_type...  17.5 us
    all_to_all x1, blocking collectives, on_device(): lax.all_to_all(score_part, 'example', split_axis=0, concat_axis=1, tiled=...  6.39 us
    all_gather x1, blocking collectives, on_device(): everyone = lax.all_gather(logged, 'example', axis=0, tiled=True)  5.24 us
    unnamed x13, local copies, waits for them, and re-layouts  4.35 us
  transfers between devices with their start and end apart: 1, of which 1 were waited for; matrix products, arithmetic and copies ran while one was open for 0% of the time, Pallas kernels for 0%

commit v1 on v0

--- a/solution.py
+++ b/solution.py
@@ -1,7 +1,14 @@
+import functools
+
 import jax
 import jax.numpy as jnp
 from jax import lax
+from jax.experimental import pallas as pl
+from jax.experimental.pallas import tpu as pltpu
 from jax.sharding import PartitionSpec as P
+
+MIB = 1 << 20
+ROWS = (((1,), (1,)), ((), ()))
 
 
 def outer_grads(left_rows, right_rows, ex_dev, seq_len, layers, proj_rank):
@@ -10,7 +17,7 @@
     return jnp.einsum("esli,eslj->elij", left_wide, right_wide, precision=lax.Precision.HIGH)
 
 
-def on_device(inputs, out_grads, lengths, proj_in, proj_out, queries):
+def on_any_mesh(inputs, out_grads, lengths, proj_in, proj_out, queries):
     layers = inputs.shape[0]
     tok_dev = inputs.shape[1]
     ex_dev = lengths.shape[0]
@@ -57,6 +64,268 @@
     return (logged, scores)
 
 
+def project_kernel(lens, x_hbm, w_hbm, o_ref, xbuf, wbuf, blocks, xsem, wsem, *, seq, masked):
+    layers, rows, _ = x_hbm.shape
+    slots, bt, _ = xbuf.shape
+    half = bt // 2
+    base = lax.axis_index("mp") * rows if masked else 0
+
+    def live_in(block):
+        row = base + block * bt
+        return lens[lax.div(row, seq)] - lax.rem(row, seq)
+
+    def add(block, count):
+        live = live_in(block) > 0
+
+        @pl.when(live)
+        def _():
+            blocks[count] = block
+
+        return count + live.astype(jnp.int32)
+
+    count = lax.fori_loop(0, rows // bt, add, jnp.int32(0))
+    total = count * layers
+
+    def place(item):
+        layer = lax.div(item, count)
+        return layer, blocks[item - layer * count]
+
+    def piece(layer, block, slot, part):
+        row = pl.multiple_of(block * bt + part * half, half)
+        return pltpu.make_async_copy(
+            x_hbm.at[layer, pl.ds(row, half)],
+            xbuf.at[slot, pl.ds(part * half, half)],
+            xsem.at[slot, part],
+        )
+
+    def fetch(item):
+        layer, block = place(item)
+        slot = lax.rem(item, slots)
+        piece(layer, block, slot, 0).start()
+
+        @pl.when(live_in(block) > half)
+        def _():
+            piece(layer, block, slot, 1).start()
+
+    def weight(layer):
+        return pltpu.make_async_copy(w_hbm.at[layer], wbuf.at[layer], wsem.at[layer])
+
+    weight(0).start()
+    for item in range(slots):
+
+        @pl.when(item < total)
+        def _():
+            fetch(jnp.int32(item))
+
+        if item == 0:
+            for layer in range(1, layers):
+                weight(layer).start()
+
+    o_ref[...] = jnp.zeros_like(o_ref)
+
+    def compute(layer, block, slot, width):
+        out = lax.dot_general(
+            wbuf[layer], xbuf[slot, :width], ROWS, preferred_element_type=jnp.float32
+        )
+        if masked:
+            at = lax.broadcasted_iota(jnp.int32, out.shape, 1)
+            out = jnp.where(at < live_in(block), out, 0.0)
+        col = pl.multiple_of(block * bt, bt)
+        o_ref[layer, :, pl.ds(col, width)] = out.astype(o_ref.dtype)
+
+    def step(item, carry):
+        layer, block = place(item)
+        slot = lax.rem(item, slots)
+        wide = live_in(block) > half
+
+        for at in range(layers):
+
+            @pl.when(item == at * count)
+            def _():
+                weight(at).wait()
+
+        piece(layer, block, slot, 0).wait()
+
+        @pl.when(wide)
+        def _():
+            piece(layer, block, slot, 1).wait()
+            compute(layer, block, slot, bt)
+
+        @pl.when(jnp.logical_not(wide))
+        def _():
+            compute(layer, block, slot, half)
+
+        @pl.when(item + slots < total)
+        def _():
+            fetch(item + slots)
+
+        return carry
+
+    lax.fori_loop(0, total, step, 0)
+
+    @pl.when(count == 0)
+    def _():
+        for layer in range(layers):
+            weight(layer).wait()
+
+
+def project(lengths, x, w, seq, masked, bt, slots, dtype):
+    layers, rows, depth = x.shape
+    rank = w.shape[1]
+    return pl.pallas_call(
+        functools.partial(project_kernel, seq=seq, masked=masked),
+        out_shape=jax.ShapeDtypeStruct((layers, rank, rows), dtype),
+        in_specs=[
+            pl.BlockSpec(memory_space=pltpu.SMEM),
+            pl.BlockSpec(memory_space=pltpu.HBM),
+            pl.BlockSpec(memory_space=pltpu.HBM),
+        ],
+        out_specs=pl.BlockSpec(memory_space=pltpu.VMEM),
+        scratch_shapes=[
+            pltpu.VMEM((slots, bt, depth), x.dtype),
+            pltpu.VMEM((layers, rank, depth), w.dtype),
+            pltpu.SMEM((rows // bt,), jnp.int32),
+            pltpu.SemaphoreType.DMA((slots, 2)),
+            pltpu.SemaphoreType.DMA((layers,)),
+        ],
+        compiler_params=pltpu.CompilerParams(vmem_limit_bytes=32 * MIB),
+        cost_estimate=pl.CostEstimate(
+            flops=2 * layers * rows * depth * 256, bytes_accessed=x.size * 2, transcendentals=0
+        ),
+    )(lengths, x, w)
+
+
+def grads_kernel(x_ref, *refs, count, seq):
+    outer, outs, (all_outer, square, cut) = refs[:count], refs[count : 2 * count], refs[2 * count :]
+    layers, rank, tokens = x_ref.shape
+    width = outer[0].shape[2]
+    me = lax.axis_index("mp")
+    for k in range(count):
+        at = pl.multiple_of(lax.bitwise_xor(me, k) * width, width)
+        all_outer[:, :, pl.ds(at, width)] = outer[k][...]
+    share_rows = cut.shape[2]
+    left = lax.broadcasted_iota(jnp.int32, (rank // 2, 2 * rank), 1) < rank
+    for e in range(tokens // seq):
+        for layer in range(layers):
+            x = x_ref[layer, :, e * seq : (e + 1) * seq]
+            high = x.astype(jnp.bfloat16)
+            low = (x - high.astype(jnp.float32)).astype(jnp.bfloat16)
+            o = all_outer[layer, :, e * seq : (e + 1) * seq]
+            both = [
+                lax.dot_general(
+                    o, jnp.concatenate([part, part], 0), ROWS, preferred_element_type=jnp.float32
+                )
+                for part in (high, low)
+            ]
+            at = e * layers + layer
+            square[at] = both[0] + both[1]
+            even = square[at, pl.ds(0, rank // 2, stride=2), :]
+            odd = square[at, pl.ds(1, rank // 2, stride=2), :]
+            flat = jnp.where(left, even, odd)
+            for row in range(0, rank // 2, share_rows):
+                share = (layer * (rank // 2) + row) // share_rows
+                cut[share, e] = flat[row : row + share_rows]
+    for k in range(count):
+        outs[k][...] = cut[lax.bitwise_xor(me, k)]
+
+
+def grads_shares(x, outer, ex_dev, seq):
+    layers, rank, tokens = x.shape
+    count = len(outer)
+    share = (ex_dev, layers * rank * rank // count // 128, 128)
+    return pl.pallas_call(
+        functools.partial(grads_kernel, count=count, seq=seq),
+        out_shape=[jax.ShapeDtypeStruct(share, jnp.float32)] * count,
+        in_specs=[pl.BlockSpec(memory_space=pltpu.VMEM)] * (count + 1),
+        out_specs=[pl.BlockSpec(memory_space=pltpu.VMEM)] * count,
+        scratch_shapes=[
+            pltpu.VMEM((layers, rank, tokens), jnp.bfloat16),
+            pltpu.VMEM((ex_dev * layers, rank, 2 * rank), jnp.float32),
+            pltpu.VMEM((count, *share), jnp.float32),
+        ],
+        compiler_params=pltpu.CompilerParams(vmem_limit_bytes=24 * MIB),
+        cost_estimate=pl.CostEstimate(flops=10**9, bytes_accessed=4 * MIB, transcendentals=0),
+    )(x, *outer)
+
+
+def scores_kernel(*refs, shares, parts):
+    share_refs, query_refs = refs[:shares], refs[shares : shares + parts]
+    logged_ref, part_ref, flat = refs[shares + parts :]
+    ex_dev, rows, lanes = share_refs[0].shape
+    me = lax.axis_index("example")
+    sums = [ref[...] for ref in share_refs]
+    while len(sums) > 1:
+        sums = [a + b for a, b in zip(sums[::2], sums[1::2])]
+    flat[...] = jnp.zeros_like(flat)
+    for e in range(ex_dev):
+        for row in range(rows):
+            flat[e : e + 1, row * lanes : (row + 1) * lanes] = sums[0][e, row : row + 1, :]
+    rounded = flat[...].astype(jnp.bfloat16)
+    logged_ref[...] = rounded[:ex_dev]
+    width = query_refs[0].shape[0]
+    for k in range(parts):
+        out = lax.dot_general(rounded, query_refs[k][...], ROWS, preferred_element_type=jnp.float32)
+        at = pl.multiple_of(lax.bitwise_xor(me, k) * width, width)
+        part_ref[:, pl.ds(at, width)] = out[:ex_dev]
+
+
+def logged_and_part(shares, queries):
+    ex_dev, rows, lanes = shares[0].shape
+    width = queries[0].shape[0] * len(queries)
+    return pl.pallas_call(
+        functools.partial(scores_kernel, shares=len(shares), parts=len(queries)),
+        out_shape=[
+            jax.ShapeDtypeStruct((ex_dev, rows * lanes), jnp.bfloat16),
+            jax.ShapeDtypeStruct((ex_dev, width), jnp.float32),
+        ],
+        in_specs=[pl.BlockSpec(memory_space=pltpu.VMEM)] * (len(shares) + len(queries)),
+        out_specs=[pl.BlockSpec(memory_space=pltpu.VMEM)] * 2,
+        scratch_shapes=[pltpu.VMEM((16, rows * lanes), jnp.float32)],
+        compiler_params=pltpu.CompilerParams(vmem_limit_bytes=24 * MIB),
+        cost_estimate=pl.CostEstimate(flops=10**9, bytes_accessed=5 * MIB, transcendentals=0),
+    )(*shares, *queries)
+
+
+def swap(x, axis, k):
+    return lax.ppermute(x, axis, [(i, i ^ k) for i in range(lax.axis_size(axis))])
+
+
+def on_device(inputs, out_grads, lengths, proj_in, proj_out, queries):
+    ex_dev = lengths.shape[0]
+    seq = inputs.shape[1] // ex_dev
+    mp = lax.axis_size("mp")
+    across = swap(queries, "example", 2)
+    mine = project(
+        lengths, out_grads, jnp.swapaxes(proj_out, 1, 2), seq, True, 256, 3, jnp.bfloat16
+    )
+    mine, later = lax.optimization_barrier((mine, lengths))
+    outer = [mine] + [swap(mine, "mp", k) for k in range(1, mp)]
+    x = project(later, inputs, jnp.swapaxes(proj_in, 1, 2), seq, False, 256, 4, jnp.float32)
+    shares = grads_shares(x, outer, ex_dev, seq)
+    shares, across = lax.optimization_barrier((shares, across))
+    all_queries = [queries, swap(queries, "example", 1), across, swap(across, "example", 1)]
+    shares = [shares[0]] + [swap(shares[k], "mp", k) for k in range(1, mp)]
+    logged, part = logged_and_part(shares, all_queries)
+    parts = [part] + [swap(part, "mp", k) for k in range(1, mp)]
+    scores = (parts[0] + parts[1]) + (parts[2] + parts[3])
+    return logged, scores
+
+
+def kernels_fit(inputs, out_grads, lengths, proj_in, mesh):
+    shape = dict(mesh.shape)
+    split = shape["groups"] * shape["example"]
+    tokens, examples = inputs.shape[1] // split, lengths.shape[0] // split
+    return (
+        shape["mp"] == 4
+        and shape["example"] == 4
+        and inputs.shape[0] == 2
+        and proj_in.shape[2] == 64
+        and examples <= 16
+        and (tokens // examples) % 256 == 0
+        and (tokens // 4) % 256 == 0
+    )
+
+
 def solution(mesh):
     placed = (
         P(None, ("groups", "example"), "mp"),
@@ -66,10 +335,15 @@
         P(),
         P("example", "mp"),
     )
-    return jax.shard_map(
-        on_device,
-        mesh=mesh,
-        in_specs=placed,
-        out_specs=(P(("groups", "example"), "mp"), P(("groups", "example"), None)),
-        check_vma=False,
-    )
+
+    def whole(inputs, out_grads, lengths, proj_in, proj_out, queries):
+        fit = kernels_fit(inputs, out_grads, lengths, proj_in, mesh)
+        return jax.shard_map(
+            on_device if fit else on_any_mesh,
+            mesh=mesh,
+            in_specs=placed,
+            out_specs=(P(("groups", "example"), "mp"), P(("groups", "example"), None)),
+            check_vma=False,
+        )(inputs, out_grads, lengths, proj_in, proj_out, queries)
+
+    return whole

time: 213 us -> 69.2 us (0.32)
  the two profiles are of different devices: /device:TPU:0 before, /device:TPU:14 now
where the time goes in v1:
time: 69.2 us; the launch traced here: 69.4 us
  Pallas kernels  45.8 us (66%)
  starting transfers between devices  13 us (19%)
  waiting for transfers between devices  7.08 us (10%)
  local copies, waits for them, and re-layouts  2.25 us (3%)
  between operations  0.73 us (1%)
    pallas_call x2, Pallas kernels, project(): pl.pallas_call(functools.partial(project_kernel, seq=seq, masked=masked),...  42.8 us
    ppermute x12, starting transfers between devices, swap(): lax.ppermute(x, axis, [(i, i ^ k) for i in range(lax.axis_size(axis))])  13 us
    ppermute x12, waiting for transfers between devices, swap(): lax.ppermute(x, axis, [(i, i ^ k) for i in range(lax.axis_size(axis))])  7.08 us
    unnamed x8, local copies, waits for them, and re-layouts  2.25 us
    pallas_call x1, Pallas kernels, logged_and_part(): pl.pallas_call(functools.partial(scores_kernel, shares=len(shares), parts...  1.7 us
  transfers between devices with their start and end apart: 12, of which 4 were waited for; matrix products, arithmetic and copies ran while one was open for 0% of the time, Pallas kernels for 47%

profile of v1, /device:TPU:14, one launch (start us, length us, event | category | flops | bytes accessed | tf_op | source)
XLA Modules:
  0.0 69.4 jit_solution(454140160281586304)
XLA Ops:
  0.6 0.0 copy-start
  0.6 1.6 %copy-done = bf16[2,8192,64]{1,2,0:T(8,128)(2,1)S(1)} copy-done((bf16[2,8192,64]{1,2,0:T(8,128)(2,1)S(1)}, bf16[2,8192,64]{1,2,0:T(8,128)(2,1)}, u32[]{:S(2)}) %copy-start) | copy-done | bytes 2097176
  2.2 0.0 copy-start.3
  2.2 0.7 copy-done.3
  2.9 0.0 copy-start.2
  2.9 0.0 copy-start.1
  2.9 11.7 %shard_map.77.refs_0_ = bf16[2,64,768]{2,1,0:T(8,128)(2,1)S(1)} custom-call(s32[3]{0:T(128)S(1)} %copy-done.3, bf16[2,768,8192]{2,1,0:T(8,128)(2,1)} %x_hbm.2, bf16[2,64,8192]{2,1,0:T(8,128)(2,1)S(1)} %bitcast.2), custom_call_target="tpu_custom_call" | custom-call | flops 6442450944 | bytes 25165824 | tf_op jit(solution)/shard_map/pallas_call | solution.py:175
  14.6 0.5 collective-permute-start
  15.1 2.2 %collective-permute-start.1 = (bf16[2,64,768]{2,1,0:T(8,128)(2,1)S(1)}, bf16[2,64,768]{2,1,0:T(8,128)(2,1)S(1)}, u32[]{:S(2)}, u32[]{:S(2)}) collective-permute-start(bf16[2,64,768]{2,1,0:T(8,128)(2,1)S(1)} %shard_map.77.refs_0_), channel_id=1, source_target_pairs={{0,8},{4,12},{8,0},{12,4},{1,9},{5,13},{9,1},{13,5},{2,10},{6,14},... | collective-permute-start | bytes 589832 | tf_op jit(solution)/shard_map/ppermute | solution.py:290
  17.4 0.8 %collective-permute-start.2 = (bf16[2,64,768]{2,1,0:T(8,128)(2,1)S(1)}, bf16[2,64,768]{2,1,0:T(8,128)(2,1)S(1)}, u32[]{:S(2)}, u32[]{:S(2)}) collective-permute-start(bf16[2,64,768]{2,1,0:T(8,128)(2,1)S(1)} %shard_map.77.refs_0_), channel_id=1, source_target_pairs={{0,12},{4,8},{8,4},{12,0},{1,13},{5,9},{9,5},{13,1},{2,14},{6,10},... | collective-permute-start | bytes 589832 | tf_op jit(solution)/shard_map/ppermute | solution.py:290
  18.2 0.0 copy-done.2
  18.2 0.0 collective-permute-start.3
  18.2 0.0 collective-permute-start.7
  18.2 0.0 copy-done.1
  18.2 31.1 %shard_map.78.x_ref = f32[2,64,3072]{2,1,0:T(8,128)S(1)} custom-call(s32[3]{0:T(128)S(1)} %copy-done.3, bf16[2,3072,7168]{2,1,0:T(8,128)(2,1)} %x_hbm.3, bf16[2,64,7168]{2,1,0:T(8,128)(2,1)S(1)} %bitcast.3), custom_call_target="tpu_custom_call" | custom-call | flops 22548578304 | bytes 88080384 | tf_op jit(solution)/shard_map/pallas_call | solution.py:175
  49.3 0.0 collective-permute-done.refs_1_
  49.3 0.0 collective-permute-done.1.refs_2_
  49.3 0.0 collective-permute-done.2.refs_3_
  49.3 1.3 %shard_map.79 = (f32[3,16,128]{2,1,0:T(8,128)S(1)}, f32[3,16,128]{2,1,0:T(8,128)S(1)}, f32[3,16,128]{2,1,0:T(8,128)S(1)}, f32[3,16,128]{2,1,0:T(8,128)S(1)}) custom-call(f32[2,64,3072]{2,1,0:T(8,128)S(1)} %shard_map.78.x_ref, bf16[2,64,768]{2,1,0:T(8,128)(2,1)S(1)} %shard_map.77.refs_0_, bf16[2,64,768]{2,1,0:T(8,128)(2,1)S(1)} %collective-permute-done.refs_1_, ...), custom_call_target="tpu_custom_call" | custom-call | flops 1000000000 | bytes 4194304 | tf_op jit(solution)/shard_map/pallas_call | solution.py:236
  50.6 0.0 collective-permute-done.3.refs_6_
  50.6 0.1 collective-permute-start.8
  50.7 1.9 %collective-permute-start.4 = (f32[3,16,128]{2,1,0:T(8,128)S(1)}, f32[3,16,128]{2,1,0:T(8,128)S(1)}, u32[]{:S(2)}, u32[]{:S(2)}) collective-permute-start(f32[3,16,128]{2,1,0:T(8,128)S(1)} %get-tuple-element.22), channel_id=1, source_target_pairs={{0,4},{4,0},{8,12},{12,8},{1,5},{5,1},{9,13},{13,9},{2,6},{6,2},{1... | collective-permute-start | bytes 73736 | tf_op jit(solution)/shard_map/ppermute | solution.py:290
  52.6 1.7 %collective-permute-start.5 = (f32[3,16,128]{2,1,0:T(8,128)S(1)}, f32[3,16,128]{2,1,0:T(8,128)S(1)}, u32[]{:S(2)}, u32[]{:S(2)}) collective-permute-start(f32[3,16,128]{2,1,0:T(8,128)S(1)} %get-tuple-element.23), channel_id=1, source_target_pairs={{0,8},{4,12},{8,0},{12,4},{1,9},{5,13},{9,1},{13,5},{2,10},{6,14},... | collective-permute-start | bytes 73736 | tf_op jit(solution)/shard_map/ppermute | solution.py:290
  54.3 0.5 collective-permute-start.6
  54.8 0.0 collective-permute-done.7.refs_5_
  54.8 0.0 collective-permute-done.4.refs_1_
  54.8 2.6 %collective-permute-done.5.refs_2_ = f32[3,16,128]{2,1,0:T(8,128)S(1)} collective-permute-done((f32[3,16,128]{2,1,0:T(8,128)S(1)}, f32[3,16,128]{2,1,0:T(8,128)S(1)}, u32[]{:S(2)}, u32[]{:S(2)}) %collective-permute-start.5) | collective-permute-done | bytes 24608 | tf_op jit(solution)/shard_map/ppermute | solution.py:290
  57.5 0.7 %collective-permute-done.6.refs_3_ = f32[3,16,128]{2,1,0:T(8,128)S(1)} collective-permute-done((f32[3,16,128]{2,1,0:T(8,128)S(1)}, f32[3,16,128]{2,1,0:T(8,128)S(1)}, u32[]{:S(2)}, u32[]{:S(2)}) %collective-permute-start.6) | collective-permute-done | bytes 24608 | tf_op jit(solution)/shard_map/ppermute | solution.py:290
  58.1 0.0 collective-permute-done.8.refs_7_
  58.2 1.7 %shard_map.80 = (bf16[3,2048]{1,0:T(4,128)(2,1)}, f32[3,1024]{1,0:T(4,128)S(1)}) custom-call(f32[3,16,128]{2,1,0:T(8,128)S(1)} %get-tuple-element.21.refs_0_, f32[3,16,128]{2,1,0:T(8,128)S(1)} %collective-permute-done.4.refs_1_, f32[3,16,128]{2,1,0:T(8,128)S(1)} %collective-permute-done.5.refs_2_, f32[3,16,128]{2,1,0:T(8,128)S(1)} %collective-permute-done.6.refs_3_, ...), custom_call_target="tpu_custom_call" | custom-call | flops 1000000000 | bytes 5242880 | tf_op jit(solution)/shard_map/pallas_call | solution.py:275
  59.9 3.0 %collective-permute-start.10 = (f32[3,1024]{1,0:T(4,128)S(1)}, f32[3,1024]{1,0:T(4,128)S(1)}, u32[]{:S(2)}, u32[]{:S(2)}) collective-permute-start(f32[3,1024]{1,0:T(4,128)S(1)} %get-tuple-element.27), channel_id=1, source_target_pairs={{0,8},{4,12},{8,0},{12,4},{1,9},{5,13},{9,1},{13,5},{2,10},{6,14},... | collective-permute-start | bytes 36872 | tf_op jit(solution)/shard_map/ppermute | solution.py:290
  62.9 2.2 %collective-permute-start.11 = (f32[3,1024]{1,0:T(4,128)S(1)}, f32[3,1024]{1,0:T(4,128)S(1)}, u32[]{:S(2)}, u32[]{:S(2)}) collective-permute-start(f32[3,1024]{1,0:T(4,128)S(1)} %get-tuple-element.27), channel_id=1, source_target_pairs={{0,12},{4,8},{8,4},{12,0},{1,13},{5,9},{9,5},{13,1},{2,14},{6,10},... | collective-permute-start | bytes 36872 | tf_op jit(solution)/shard_map/ppermute | solution.py:290
  65.1 0.0 collective-permute-start.9
  65.1 0.0 collective-permute-done.10
  65.1 1.9 %collective-permute-done.11 = f32[3,1024]{1,0:T(4,128)S(1)} collective-permute-done((f32[3,1024]{1,0:T(4,128)S(1)}, f32[3,1024]{1,0:T(4,128)S(1)}, u32[]{:S(2)}, u32[]{:S(2)}) %collective-permute-start.11) | collective-permute-done | bytes 12320 | tf_op jit(solution)/shard_map/ppermute | solution.py:290
  66.9 1.9 %collective-permute-done.9 = f32[3,1024]{1,0:T(4,128)S(1)} collective-permute-done((f32[3,1024]{1,0:T(4,128)S(1)}, f32[3,1024]{1,0:T(4,128)S(1)}, u32[]{:S(2)}, u32[]{:S(2)}) %collective-permute-start.9) | collective-permute-done | bytes 12320 | tf_op jit(solution)/shard_map/ppermute | solution.py:290
  68.8 0.6 add_add_fusion
Async XLA Ops:
  0.6 1.6 %copy-start = (bf16[2,8192,64]{1,2,0:T(8,128)(2,1)S(1)}, bf16[2,8192,64]{1,2,0:T(8,128)(2,1)}, u32[]{:S(2)}) copy-start(bf16[2,8192,64]{1,2,0:T(8,128)(2,1)} %param.10) | copy-start | bytes 6291460
  2.2 0.7 copy-start.3
  2.9 15.3 %copy-start.2 = (bf16[256,2048]{1,0:T(8,128)(2,1)S(1)}, bf16[256,2048]{1,0:T(8,128)(2,1)}, u32[]{:S(2)}) copy-start(bf16[256,2048]{1,0:T(8,128)(2,1)} %refs_4_.1) | copy-start | bytes 3145732
  2.9 15.3 %copy-start.1 = (bf16[2,7168,64]{1,2,0:T(8,128)(2,1)S(1)}, bf16[2,7168,64]{1,2,0:T(8,128)(2,1)}, u32[]{:S(2)}) copy-start(bf16[2,7168,64]{1,2,0:T(8,128)(2,1)} %param.9) | copy-start | bytes 5505028
  14.6 34.7 %collective-permute-start = (bf16[2,64,768]{2,1,0:T(8,128)(2,1)S(1)}, bf16[2,64,768]{2,1,0:T(8,128)(2,1)S(1)}, u32[]{:S(2)}, u32[]{:S(2)}) collective-permute-start(bf16[2,64,768]{2,1,0:T(8,128)(2,1)S(1)} %shard_map.77.refs_0_), channel_id=1, source_target_pairs={{0,4},{4,0},{8,12},{12,8},{1,5},{5,1},{9,13},{13,9},{2,6},{6,2},{1... | collective-permute-start | bytes 589832 | tf_op jit(solution)/shard_map/ppermute | solution.py:290
  15.1 34.2 %collective-permute-start.1 = (bf16[2,64,768]{2,1,0:T(8,128)(2,1)S(1)}, bf16[2,64,768]{2,1,0:T(8,128)(2,1)S(1)}, u32[]{:S(2)}, u32[]{:S(2)}) collective-permute-start(bf16[2,64,768]{2,1,0:T(8,128)(2,1)S(1)} %shard_map.77.refs_0_), channel_id=1, source_target_pairs={{0,8},{4,12},{8,0},{12,4},{1,9},{5,13},{9,1},{13,5},{2,10},{6,14},... | collective-permute-start | bytes 589832 | tf_op jit(solution)/shard_map/ppermute | solution.py:290
  17.4 32.0 %collective-permute-start.2 = (bf16[2,64,768]{2,1,0:T(8,128)(2,1)S(1)}, bf16[2,64,768]{2,1,0:T(8,128)(2,1)S(1)}, u32[]{:S(2)}, u32[]{:S(2)}) collective-permute-start(bf16[2,64,768]{2,1,0:T(8,128)(2,1)S(1)} %shard_map.77.refs_0_), channel_id=1, source_target_pairs={{0,12},{4,8},{8,4},{12,0},{1,13},{5,9},{9,5},{13,1},{2,14},{6,10},... | collective-permute-start | bytes 589832 | tf_op jit(solution)/shard_map/ppermute | solution.py:290
  18.2 32.4 %collective-permute-start.3 = (bf16[256,2048]{1,0:T(8,128)(2,1)S(1)}, bf16[256,2048]{1,0:T(8,128)(2,1)S(1)}, u32[]{:S(2)}, u32[]{:S(2)}) collective-permute-start(bf16[256,2048]{1,0:T(8,128)(2,1)S(1)} %copy-done.2), channel_id=1, source_target_pairs={{0,2},{1,3},{2,0},{3,1},{4,6},{5,7},{6,4},{7,5},{8,10},{9,11},{10,... | collective-permute-start | bytes 3145736 | tf_op jit(solution)/shard_map/ppermute | solution.py:290
  18.2 36.6 %collective-permute-start.7 = (bf16[256,2048]{1,0:T(8,128)(2,1)S(1)}, bf16[256,2048]{1,0:T(8,128)(2,1)S(1)}, u32[]{:S(2)}, u32[]{:S(2)}) collective-permute-start(bf16[256,2048]{1,0:T(8,128)(2,1)S(1)} %copy-done.2), channel_id=1, source_target_pairs={{0,1},{1,0},{2,3},{3,2},{4,5},{5,4},{6,7},{7,6},{8,9},{9,8},{10,11... | collective-permute-start | bytes 3145736 | tf_op jit(solution)/shard_map/ppermute | solution.py:290
  50.6 7.5 %collective-permute-start.8 = (bf16[256,2048]{1,0:T(8,128)(2,1)S(1)}, bf16[256,2048]{1,0:T(8,128)(2,1)S(1)}, u32[]{:S(2)}, u32[]{:S(2)}) collective-permute-start(bf16[256,2048]{1,0:T(8,128)(2,1)S(1)} %collective-permute-done.3.refs_6_), channel_id=1, source_target_pairs={{0,1},{1,0},{2,3},{3,2},{4,5},{5,4},{6,7},{7,6},{8,9},{9,8},{10,11... | collective-permute-start | bytes 3145736 | tf_op jit(solution)/shard_map/ppermute | solution.py:290
  50.7 4.1 %collective-permute-start.4 = (f32[3,16,128]{2,1,0:T(8,128)S(1)}, f32[3,16,128]{2,1,0:T(8,128)S(1)}, u32[]{:S(2)}, u32[]{:S(2)}) collective-permute-start(f32[3,16,128]{2,1,0:T(8,128)S(1)} %get-tuple-element.22), channel_id=1, source_target_pairs={{0,4},{4,0},{8,12},{12,8},{1,5},{5,1},{9,13},{13,9},{2,6},{6,2},{1... | collective-permute-start | bytes 73736 | tf_op jit(solution)/shard_map/ppermute | solution.py:290
  52.6 4.8 %collective-permute-start.5 = (f32[3,16,128]{2,1,0:T(8,128)S(1)}, f32[3,16,128]{2,1,0:T(8,128)S(1)}, u32[]{:S(2)}, u32[]{:S(2)}) collective-permute-start(f32[3,16,128]{2,1,0:T(8,128)S(1)} %get-tuple-element.23), channel_id=1, source_target_pairs={{0,8},{4,12},{8,0},{12,4},{1,9},{5,13},{9,1},{13,5},{2,10},{6,14},... | collective-permute-start | bytes 73736 | tf_op jit(solution)/shard_map/ppermute | solution.py:290
  54.3 3.8 %collective-permute-start.6 = (f32[3,16,128]{2,1,0:T(8,128)S(1)}, f32[3,16,128]{2,1,0:T(8,128)S(1)}, u32[]{:S(2)}, u32[]{:S(2)}) collective-permute-start(f32[3,16,128]{2,1,0:T(8,128)S(1)} %get-tuple-element.24), channel_id=1, source_target_pairs={{0,12},{4,8},{8,4},{12,0},{1,13},{5,9},{9,5},{13,1},{2,14},{6,10},... | collective-permute-start | bytes 73736 | tf_op jit(solution)/shard_map/ppermute | solution.py:290
  59.9 5.2 %collective-permute-start.10 = (f32[3,1024]{1,0:T(4,128)S(1)}, f32[3,1024]{1,0:T(4,128)S(1)}, u32[]{:S(2)}, u32[]{:S(2)}) collective-permute-start(f32[3,1024]{1,0:T(4,128)S(1)} %get-tuple-element.27), channel_id=1, source_target_pairs={{0,8},{4,12},{8,0},{12,4},{1,9},{5,13},{9,1},{13,5},{2,10},{6,14},... | collective-permute-start | bytes 36872 | tf_op jit(solution)/shard_map/ppermute | solution.py:290
  62.9 4.1 %collective-permute-start.11 = (f32[3,1024]{1,0:T(4,128)S(1)}, f32[3,1024]{1,0:T(4,128)S(1)}, u32[]{:S(2)}, u32[]{:S(2)}) collective-permute-start(f32[3,1024]{1,0:T(4,128)S(1)} %get-tuple-element.27), channel_id=1, source_target_pairs={{0,12},{4,8},{8,4},{12,0},{1,13},{5,9},{9,5},{13,1},{2,14},{6,10},... | collective-permute-start | bytes 36872 | tf_op jit(solution)/shard_map/ppermute | solution.py:290
  65.1 3.7 %collective-permute-start.9 = (f32[3,1024]{1,0:T(4,128)S(1)}, f32[3,1024]{1,0:T(4,128)S(1)}, u32[]{:S(2)}, u32[]{:S(2)}) collective-permute-start(f32[3,1024]{1,0:T(4,128)S(1)} %get-tuple-element.27), channel_id=1, source_target_pairs={{0,4},{4,0},{8,12},{12,8},{1,5},{5,1},{9,13},{13,9},{2,6},{6,2},{1... | collective-permute-start | bytes 36872 | tf_op jit(solution)/shard_map/ppermute | solution.py:290

commit v2 on v1

--- a/solution.py
+++ b/solution.py
@@ -64,131 +64,145 @@
     return (logged, scores)
 
 
-def project_kernel(lens, x_hbm, w_hbm, o_ref, xbuf, wbuf, blocks, xsem, wsem, *, seq, masked):
+def project_kernel(lens_hbm, x_hbm, w_hbm, o_ref, xbuf, wbuf, sums, lens, places, xsem, wsem, lsem, *, seq, masked):
     layers, rows, _ = x_hbm.shape
-    slots, bt, _ = xbuf.shape
-    half = bt // 2
+    rank = w_hbm.shape[1]
+    slots, chunk, _ = xbuf.shape
+    most = xsem.shape[1]
+    granule = chunk // most
+    half = most // 2
     base = lax.axis_index("mp") * rows if masked else 0
 
-    def live_in(block):
-        row = base + block * bt
-        return lens[lax.div(row, seq)] - lax.rem(row, seq)
-
-    def add(block, count):
-        live = live_in(block) > 0
-
-        @pl.when(live)
+    lens_copy = pltpu.make_async_copy(lens_hbm, lens, lsem)
+    lens_copy.start()
+    weights = [
+        pltpu.make_async_copy(w_hbm.at[layer], wbuf.at[pl.ds(layer * rank, rank)], wsem.at[layer])
+        for layer in range(layers)
+    ]
+    for copy in weights:
+        copy.start()
+    lens_copy.wait()
+
+    spans = []
+    count = jnp.int32(0)
+    for e in range(lens.shape[0]):
+        low = jnp.clip(e * seq - base, 0, rows)
+        high = jnp.clip(e * seq + lens[e] - base, 0, rows)
+        here = lax.shift_right_logical(jnp.maximum(high - low, 0) + (granule - 1), granule.bit_length() - 1)
+
+        def put(i, carry, low=low, at=count):
+            places[at + i] = low + i * granule
+            return carry
+
+        lax.fori_loop(0, here, put, 0)
+        count = count + here
+        spans.append((low, high))
+    total = count * layers
+
+    def place(item):
+        layer = (item >= count).astype(jnp.int32)
+        return layer, pl.multiple_of(places[item - layer * count], granule)
+
+    def in_chunk(c):
+        first = jnp.maximum(c * most - half, 0)
+        return first, jnp.minimum(jnp.where(c == 0, half, most), total - first)
+
+    chunks = lax.shift_right_logical(total + half + most - 1, most.bit_length() - 1)
+    chunks = jnp.where(total > 0, chunks, 0)
+
+    def piece(item, slot, g):
+        layer, row = place(item)
+        return pltpu.make_async_copy(
+            x_hbm.at[layer, pl.ds(row, granule)],
+            xbuf.at[slot, pl.ds(g * granule, granule)],
+            xsem.at[slot, g],
+        )
+
+    def each(c, slot, start):
+        first, n = in_chunk(c)
+        for g in range(most):
+
+            @pl.when(g < n)
+            def _():
+                copy = piece(first + g, slot, g)
+                copy.start() if start else copy.wait()
+
+    for c in range(slots):
+
+        @pl.when(c < chunks)
         def _():
-            blocks[count] = block
-
-        return count + live.astype(jnp.int32)
-
-    count = lax.fori_loop(0, rows // bt, add, jnp.int32(0))
-    total = count * layers
-
-    def place(item):
-        layer = lax.div(item, count)
-        return layer, blocks[item - layer * count]
-
-    def piece(layer, block, slot, part):
-        row = pl.multiple_of(block * bt + part * half, half)
-        return pltpu.make_async_copy(
-            x_hbm.at[layer, pl.ds(row, half)],
-            xbuf.at[slot, pl.ds(part * half, half)],
-            xsem.at[slot, part],
+            each(jnp.int32(c), c, True)
+
+    sums[...] = jnp.zeros_like(sums)
+    for copy in weights:
+        copy.wait()
+    second = lax.broadcasted_iota(jnp.int32, (granule, layers * rank), 1) // rank
+
+    def compute(c, slot, parts):
+        first, n = in_chunk(c)
+        out = lax.dot_general(
+            xbuf[slot, : parts * granule], wbuf[...], ROWS, preferred_element_type=jnp.float32
         )
-
-    def fetch(item):
-        layer, block = place(item)
-        slot = lax.rem(item, slots)
-        piece(layer, block, slot, 0).start()
-
-        @pl.when(live_in(block) > half)
+        for g in range(parts):
+            layer, row = place(jnp.minimum(first + g, total - 1))
+            row = pl.multiple_of(jnp.where(g < n, row, rows), granule)
+            at = pl.ds(row, granule)
+            sums[at, :] = jnp.where(second == layer, out[g * granule : (g + 1) * granule], sums[at, :])
+
+    def step(c, slot):
+        each(c, slot, False)
+        n = in_chunk(c)[1]
+        pl.when(n <= half)(functools.partial(compute, c, slot, half))
+        pl.when(n > half)(functools.partial(compute, c, slot, most))
+
+        @pl.when(c + slots < chunks)
         def _():
-            piece(layer, block, slot, 1).start()
-
-    def weight(layer):
-        return pltpu.make_async_copy(w_hbm.at[layer], wbuf.at[layer], wsem.at[layer])
-
-    weight(0).start()
-    for item in range(slots):
-
-        @pl.when(item < total)
-        def _():
-            fetch(jnp.int32(item))
-
-        if item == 0:
-            for layer in range(1, layers):
-                weight(layer).start()
-
-    o_ref[...] = jnp.zeros_like(o_ref)
-
-    def compute(layer, block, slot, width):
-        out = lax.dot_general(
-            wbuf[layer], xbuf[slot, :width], ROWS, preferred_element_type=jnp.float32
-        )
-        if masked:
-            at = lax.broadcasted_iota(jnp.int32, out.shape, 1)
-            out = jnp.where(at < live_in(block), out, 0.0)
-        col = pl.multiple_of(block * bt, bt)
-        o_ref[layer, :, pl.ds(col, width)] = out.astype(o_ref.dtype)
-
-    def step(item, carry):
-        layer, block = place(item)
-        slot = lax.rem(item, slots)
-        wide = live_in(block) > half
-
-        for at in range(layers):
-
-            @pl.when(item == at * count)
-            def _():
-                weight(at).wait()
-
-        piece(layer, block, slot, 0).wait()
-
-        @pl.when(wide)
-        def _():
-            piece(layer, block, slot, 1).wait()
-            compute(layer, block, slot, bt)
-
-        @pl.when(jnp.logical_not(wide))
-        def _():
-            compute(layer, block, slot, half)
-
-        @pl.when(item + slots < total)
-        def _():
-            fetch(item + slots)
-
-        return carry
-
-    lax.fori_loop(0, total, step, 0)
-
-    @pl.when(count == 0)
-    def _():
-        for layer in range(layers):
-            weight(layer).wait()
-
-
-def project(lengths, x, w, seq, masked, bt, slots, dtype):
+            each(c + slots, slot, True)
+
+        return jnp.where(slot + 1 == slots, 0, slot + 1)
+
+    lax.fori_loop(0, chunks, step, jnp.int32(0))
+    if masked:
+        turned = sums[:rows].T
+        token = lax.broadcasted_iota(jnp.int32, turned.shape, 1)
+        live = token < 0
+        for low, high in spans:
+            live = live | ((token >= low) & (token < high))
+        o_ref[...] = jnp.where(live, turned, 0.0).astype(o_ref.dtype)
+
+
+def project(lengths, x, w, seq, masked, chunk, granule, slots, limit):
     layers, rows, depth = x.shape
     rank = w.shape[1]
+    wide = layers * rank
+    summed = (rows + granule, wide)
+    if masked:
+        out = jax.ShapeDtypeStruct((wide, rows), jnp.bfloat16)
+        body = project_kernel
+        more = [pltpu.VMEM(summed, jnp.float32)]
+    else:
+        out = jax.ShapeDtypeStruct(summed, jnp.float32)
+        more = []
+
+        def body(lens_hbm, x_hbm, w_hbm, o_ref, xbuf, wbuf, *rest, **options):
+            project_kernel(lens_hbm, x_hbm, w_hbm, o_ref, xbuf, wbuf, o_ref, *rest, **options)
+
     return pl.pallas_call(
-        functools.partial(project_kernel, seq=seq, masked=masked),
-        out_shape=jax.ShapeDtypeStruct((layers, rank, rows), dtype),
-        in_specs=[
-            pl.BlockSpec(memory_space=pltpu.SMEM),
-            pl.BlockSpec(memory_space=pltpu.HBM),
-            pl.BlockSpec(memory_space=pltpu.HBM),
-        ],
+        functools.partial(body, seq=seq, masked=masked),
+        out_shape=out,
+        in_specs=[pl.BlockSpec(memory_space=pltpu.HBM)] * 3,
         out_specs=pl.BlockSpec(memory_space=pltpu.VMEM),
         scratch_shapes=[
-            pltpu.VMEM((slots, bt, depth), x.dtype),
-            pltpu.VMEM((layers, rank, depth), w.dtype),
-            pltpu.SMEM((rows // bt,), jnp.int32),
-            pltpu.SemaphoreType.DMA((slots, 2)),
+            pltpu.VMEM((slots, chunk, depth), x.dtype),
+            pltpu.VMEM((wide, depth), w.dtype),
+            *more,
+            pltpu.SMEM(lengths.shape, jnp.int32),
+            pltpu.SMEM((rows // granule,), jnp.int32),
+            pltpu.SemaphoreType.DMA((slots, chunk // granule)),
             pltpu.SemaphoreType.DMA((layers,)),
+            pltpu.SemaphoreType.DMA,
         ],
-        compiler_params=pltpu.CompilerParams(vmem_limit_bytes=32 * MIB),
+        compiler_params=pltpu.CompilerParams(vmem_limit_bytes=limit * MIB),
         cost_estimate=pl.CostEstimate(
             flops=2 * layers * rows * depth * 256, bytes_accessed=x.size * 2, transcendentals=0
         ),
@@ -197,30 +211,29 @@
 
 def grads_kernel(x_ref, *refs, count, seq):
     outer, outs, (all_outer, square, cut) = refs[:count], refs[count : 2 * count], refs[2 * count :]
-    layers, rank, tokens = x_ref.shape
-    width = outer[0].shape[2]
+    wide, width = outer[0].shape
+    examples, rank = cut.shape[1], wide // 2
     me = lax.axis_index("mp")
     for k in range(count):
         at = pl.multiple_of(lax.bitwise_xor(me, k) * width, width)
-        all_outer[:, :, pl.ds(at, width)] = outer[k][...]
+        all_outer[:, pl.ds(at, width)] = outer[k][...]
     share_rows = cut.shape[2]
-    left = lax.broadcasted_iota(jnp.int32, (rank // 2, 2 * rank), 1) < rank
-    for e in range(tokens // seq):
-        for layer in range(layers):
-            x = x_ref[layer, :, e * seq : (e + 1) * seq]
-            high = x.astype(jnp.bfloat16)
-            low = (x - high.astype(jnp.float32)).astype(jnp.bfloat16)
-            o = all_outer[layer, :, e * seq : (e + 1) * seq]
-            both = [
-                lax.dot_general(
-                    o, jnp.concatenate([part, part], 0), ROWS, preferred_element_type=jnp.float32
-                )
-                for part in (high, low)
-            ]
-            at = e * layers + layer
-            square[at] = both[0] + both[1]
-            even = square[at, pl.ds(0, rank // 2, stride=2), :]
-            odd = square[at, pl.ds(1, rank // 2, stride=2), :]
+    left = lax.broadcasted_iota(jnp.int32, (rank // 2, wide), 1) < rank
+    for e in range(examples):
+        x = x_ref[e * seq : (e + 1) * seq, :]
+        high = x.astype(jnp.bfloat16)
+        low = (x - high.astype(jnp.float32)).astype(jnp.bfloat16)
+        o = all_outer[:, e * seq : (e + 1) * seq]
+        square[e] = jnp.dot(o, high, preferred_element_type=jnp.float32) + jnp.dot(
+            o, low, preferred_element_type=jnp.float32
+        )
+        for layer in range(2):
+            even = square[e, pl.ds(layer * rank, rank // 2, stride=2), :]
+            odd = square[e, pl.ds(layer * rank + 1, rank // 2, stride=2), :]
+            if layer == 0:
+                odd = pltpu.roll(odd, rank, 1)
+            else:
+                even = pltpu.roll(even, rank, 1)
             flat = jnp.where(left, even, odd)
             for row in range(0, rank // 2, share_rows):
                 share = (layer * (rank // 2) + row) // share_rows
@@ -230,20 +243,20 @@
 
 
 def grads_shares(x, outer, ex_dev, seq):
-    layers, rank, tokens = x.shape
+    wide = x.shape[1]
     count = len(outer)
-    share = (ex_dev, layers * rank * rank // count // 128, 128)
+    share = (ex_dev, wide * wide // 2 // count // 128, 128)
     return pl.pallas_call(
         functools.partial(grads_kernel, count=count, seq=seq),
         out_shape=[jax.ShapeDtypeStruct(share, jnp.float32)] * count,
         in_specs=[pl.BlockSpec(memory_space=pltpu.VMEM)] * (count + 1),
         out_specs=[pl.BlockSpec(memory_space=pltpu.VMEM)] * count,
         scratch_shapes=[
-            pltpu.VMEM((layers, rank, tokens), jnp.bfloat16),
-            pltpu.VMEM((ex_dev * layers, rank, 2 * rank), jnp.float32),
+            pltpu.VMEM((wide, ex_dev * seq), jnp.bfloat16),
+            pltpu.VMEM((ex_dev, wide, wide), jnp.float32),
             pltpu.VMEM((count, *share), jnp.float32),
         ],
-        compiler_params=pltpu.CompilerParams(vmem_limit_bytes=24 * MIB),
+        compiler_params=pltpu.CompilerParams(vmem_limit_bytes=16 * MIB),
         cost_estimate=pl.CostEstimate(flops=10**9, bytes_accessed=4 * MIB, transcendentals=0),
     )(x, *outer)
 
@@ -295,15 +308,13 @@
     seq = inputs.shape[1] // ex_dev
     mp = lax.axis_size("mp")
     across = swap(queries, "example", 2)
-    mine = project(
-        lengths, out_grads, jnp.swapaxes(proj_out, 1, 2), seq, True, 256, 3, jnp.bfloat16
-    )
+    mine = project(lengths, out_grads, jnp.swapaxes(proj_out, 1, 2), seq, True, 256, 64, 3, 60)
     mine, later = lax.optimization_barrier((mine, lengths))
     outer = [mine] + [swap(mine, "mp", k) for k in range(1, mp)]
-    x = project(later, inputs, jnp.swapaxes(proj_in, 1, 2), seq, False, 256, 4, jnp.float32)
+    x = project(later, inputs, jnp.swapaxes(proj_in, 1, 2), seq, False, 512, 64, 3, 32)
+    x, across, *outer = lax.optimization_barrier((x, across, *outer))
+    all_queries = [queries, swap(queries, "example", 1), across, swap(across, "example", 1)]
     shares = grads_shares(x, outer, ex_dev, seq)
-    shares, across = lax.optimization_barrier((shares, across))
-    all_queries = [queries, swap(queries, "example", 1), across, swap(across, "example", 1)]
     shares = [shares[0]] + [swap(shares[k], "mp", k) for k in range(1, mp)]
     logged, part = logged_and_part(shares, all_queries)
     parts = [part] + [swap(part, "mp", k) for k in range(1, mp)]

time: 69.2 us -> 64.5 us (0.932)
  the two profiles are of different devices: /device:TPU:14 before, /device:TPU:0 now
where the time goes in v2:
time: 64.5 us; the launch traced here: 63.5 us
  Pallas kernels  39.4 us (61%)
  starting transfers between devices  16.4 us (25%)
  waiting for transfers between devices  6.34 us (10%)
  between operations  0.74 us (1%)
    pallas_call x2, Pallas kernels, project(): pl.pallas_call(functools.partial(body, seq=seq, masked=masked), out_shape...  36.9 us
    ppermute x12, starting transfers between devices, swap(): lax.ppermute(x, axis, [(i, i ^ k) for i in range(lax.axis_size(axis))])  16.4 us
    ppermute x12, waiting for transfers between devices, swap(): lax.ppermute(x, axis, [(i, i ^ k) for i in range(lax.axis_size(axis))])  6.34 us
    pallas_call x1, Pallas kernels, logged_and_part(): pl.pallas_call(functools.partial(scores_kernel, shares=len(shares), parts...  1.7 us
  transfers between devices with their start and end apart: 12, of which 4 were waited for; matrix products, arithmetic and copies ran while one was open for 0% of the time, Pallas kernels for 42%

profile of v2, /device:TPU:0, one launch (start us, length us, event | category | flops | bytes accessed | tf_op | source)
XLA Modules:
  0.0 63.5 jit_solution(5878736339103351298)
XLA Ops:
  0.6 0.0 copy-start.1
  0.6 0.0 copy-start
  0.7 0.0 copy-start.3
  0.7 11.1 %shard_map.77.refs_0_ = bf16[128,768]{1,0:T(8,128)(2,1)} custom-call(s32[3]{0:T(128)} %lens_hbm.2, bf16[2,768,8192]{2,1,0:T(8,128)(2,1)} %x_hbm.2, bf16[2,64,8192]{2,1,0:T(8,128)(2,1)} %bitcast.3), custom_call_target="tpu_custom_call" | custom-call | flops 6442450944 | bytes 25165824 | tf_op jit(solution)/shard_map/pallas_call | solution.py:190
  11.8 1.8 %collective-permute-start.1 = (bf16[128,768]{1,0:T(8,128)(2,1)}, bf16[128,768]{1,0:T(8,128)(2,1)S(1)}, u32[]{:S(2)}, u32[]{:S(2)}) collective-permute-start(bf16[128,768]{1,0:T(8,128)(2,1)} %shard_map.77.refs_0_), channel_id=1, source_target_pairs={{0,4},{4,0},{8,12},{12,8},{1,5},{5,1},{9,13},{13,9},{2,6},{6,2},{1... | collective-permute-start | bytes 589832 | tf_op jit(solution)/shard_map/ppermute | solution.py:303
  13.6 5.2 %collective-permute-start.2 = (bf16[128,768]{1,0:T(8,128)(2,1)}, bf16[128,768]{1,0:T(8,128)(2,1)S(1)}, u32[]{:S(2)}, u32[]{:S(2)}) collective-permute-start(bf16[128,768]{1,0:T(8,128)(2,1)} %shard_map.77.refs_0_), channel_id=1, source_target_pairs={{0,8},{4,12},{8,0},{12,4},{1,9},{5,13},{9,1},{13,5},{2,10},{6,14},... | collective-permute-start | bytes 589832 | tf_op jit(solution)/shard_map/ppermute | solution.py:303
  18.8 0.0 collective-permute-start.3
  18.8 0.0 copy-done.1
  18.8 1.4 %collective-permute-start = (bf16[256,2048]{1,0:T(8,128)(2,1)S(1)}, bf16[256,2048]{1,0:T(8,128)(2,1)S(1)}, u32[]{:S(2)}, u32[]{:S(2)}) collective-permute-start(bf16[256,2048]{1,0:T(8,128)(2,1)S(1)} %copy-done.1), channel_id=1, source_target_pairs={{0,2},{1,3},{2,0},{3,1},{4,6},{5,7},{6,4},{7,5},{8,10},{9,11},{10,... | collective-permute-start | bytes 3145736 | tf_op jit(solution)/shard_map/ppermute | solution.py:303
  20.2 0.0 collective-permute-start.7
  20.2 0.0 copy-done
  20.2 0.0 copy-done.3
  20.2 0.0 copy-start.2
  20.2 25.8 %shard_map.78.x_ref = f32[3136,128]{1,0:T(8,128)S(1)} custom-call(s32[3]{0:T(128)S(1)} %copy-done.3, bf16[2,3072,7168]{2,1,0:T(8,128)(2,1)} %x_hbm.3, bf16[2,64,7168]{2,1,0:T(8,128)(2,1)S(1)} %bitcast.2), custom_call_target="tpu_custom_call" | custom-call | flops 22548578304 | bytes 88080384 | tf_op jit(solution)/shard_map/pallas_call | solution.py:190
  46.0 0.0 collective-permute-done.1.refs_1_
  46.0 0.0 collective-permute-done.2.refs_2_
  46.0 0.0 collective-permute-done.3.refs_3_
  46.1 0.0 collective-permute-done.refs_6_
  46.1 0.1 collective-permute-start.8
  46.1 0.0 copy-done.2
  46.1 0.7 %shard_map.79 = (f32[3,16,128]{2,1,0:T(8,128)S(1)}, f32[3,16,128]{2,1,0:T(8,128)S(1)}, f32[3,16,128]{2,1,0:T(8,128)S(1)}, f32[3,16,128]{2,1,0:T(8,128)S(1)}) custom-call(f32[3136,128]{1,0:T(8,128)S(1)} %shard_map.78.x_ref, bf16[128,768]{1,0:T(8,128)(2,1)S(1)} %copy-done.2, bf16[128,768]{1,0:T(8,128)(2,1)S(1)} %collective-permute-done.1.refs_1_, ...), custom_call_target="tpu_custom_call" | custom-call | flops 1000000000 | bytes 4194304 | tf_op jit(solution)/shard_map/pallas_call | solution.py:249
  46.9 0.6 collective-permute-start.4
  47.5 2.5 %collective-permute-start.5 = (f32[3,16,128]{2,1,0:T(8,128)S(1)}, f32[3,16,128]{2,1,0:T(8,128)S(1)}, u32[]{:S(2)}, u32[]{:S(2)}) collective-permute-start(f32[3,16,128]{2,1,0:T(8,128)S(1)} %get-tuple-element.25), channel_id=1, source_target_pairs={{0,8},{4,12},{8,0},{12,4},{1,9},{5,13},{9,1},{13,5},{2,10},{6,14},... | collective-permute-start | bytes 73736 | tf_op jit(solution)/shard_map/ppermute | solution.py:303
  50.0 1.4 %collective-permute-start.6 = (f32[3,16,128]{2,1,0:T(8,128)S(1)}, f32[3,16,128]{2,1,0:T(8,128)S(1)}, u32[]{:S(2)}, u32[]{:S(2)}) collective-permute-start(f32[3,16,128]{2,1,0:T(8,128)S(1)} %get-tuple-element.26), channel_id=1, source_target_pairs={{0,12},{4,8},{8,4},{12,0},{1,13},{5,9},{9,5},{13,1},{2,14},{6,10},... | collective-permute-start | bytes 73736 | tf_op jit(solution)/shard_map/ppermute | solution.py:303
  51.3 0.0 collective-permute-done.7.refs_5_
  51.4 0.0 collective-permute-done.4.refs_1_
  51.4 1.0 %collective-permute-done.5.refs_2_ = f32[3,16,128]{2,1,0:T(8,128)S(1)} collective-permute-done((f32[3,16,128]{2,1,0:T(8,128)S(1)}, f32[3,16,128]{2,1,0:T(8,128)S(1)}, u32[]{:S(2)}, u32[]{:S(2)}) %collective-permute-start.5) | collective-permute-done | bytes 24608 | tf_op jit(solution)/shard_map/ppermute | solution.py:303
  52.4 3.2 %collective-permute-done.6.refs_3_ = f32[3,16,128]{2,1,0:T(8,128)S(1)} collective-permute-done((f32[3,16,128]{2,1,0:T(8,128)S(1)}, f32[3,16,128]{2,1,0:T(8,128)S(1)}, u32[]{:S(2)}, u32[]{:S(2)}) %collective-permute-start.6) | collective-permute-done | bytes 24608 | tf_op jit(solution)/shard_map/ppermute | solution.py:303
  55.6 0.0 collective-permute-done.8.refs_7_
  55.6 1.7 %shard_map.80 = (bf16[3,2048]{1,0:T(4,128)(2,1)}, f32[3,1024]{1,0:T(4,128)S(1)}) custom-call(f32[3,16,128]{2,1,0:T(8,128)S(1)} %get-tuple-element.23.refs_0_, f32[3,16,128]{2,1,0:T(8,128)S(1)} %collective-permute-done.4.refs_1_, f32[3,16,128]{2,1,0:T(8,128)S(1)} %collective-permute-done.5.refs_2_, f32[3,16,128]{2,1,0:T(8,128)S(1)} %collective-permute-done.6.refs_3_, ...), custom_call_target="tpu_custom_call" | custom-call | flops 1000000000 | bytes 5242880 | tf_op jit(solution)/shard_map/pallas_call | solution.py:288
  57.3 0.0 collective-permute-start.10
  57.3 1.6 %collective-permute-start.11 = (f32[3,1024]{1,0:T(4,128)S(1)}, f32[3,1024]{1,0:T(4,128)S(1)}, u32[]{:S(2)}, u32[]{:S(2)}) collective-permute-start(f32[3,1024]{1,0:T(4,128)S(1)} %get-tuple-element.29), channel_id=1, source_target_pairs={{0,12},{4,8},{8,4},{12,0},{1,13},{5,9},{9,5},{13,1},{2,14},{6,10},... | collective-permute-start | bytes 36872 | tf_op jit(solution)/shard_map/ppermute | solution.py:303
  58.9 1.9 %collective-permute-start.9 = (f32[3,1024]{1,0:T(4,128)S(1)}, f32[3,1024]{1,0:T(4,128)S(1)}, u32[]{:S(2)}, u32[]{:S(2)}) collective-permute-start(f32[3,1024]{1,0:T(4,128)S(1)} %get-tuple-element.29), channel_id=1, source_target_pairs={{0,4},{4,0},{8,12},{12,8},{1,5},{5,1},{9,13},{13,9},{2,6},{6,2},{1... | collective-permute-start | bytes 36872 | tf_op jit(solution)/shard_map/ppermute | solution.py:303
  60.8 1.1 %collective-permute-done.10 = f32[3,1024]{1,0:T(4,128)S(1)} collective-permute-done((f32[3,1024]{1,0:T(4,128)S(1)}, f32[3,1024]{1,0:T(4,128)S(1)}, u32[]{:S(2)}, u32[]{:S(2)}) %collective-permute-start.10) | collective-permute-done | bytes 12320 | tf_op jit(solution)/shard_map/ppermute | solution.py:303
  62.0 0.9 %collective-permute-done.11 = f32[3,1024]{1,0:T(4,128)S(1)} collective-permute-done((f32[3,1024]{1,0:T(4,128)S(1)}, f32[3,1024]{1,0:T(4,128)S(1)}, u32[]{:S(2)}, u32[]{:S(2)}) %collective-permute-start.11) | collective-permute-done | bytes 12320 | tf_op jit(solution)/shard_map/ppermute | solution.py:303
  62.9 0.0 collective-permute-done.9
  62.9 0.6 add_add_fusion
Async XLA Ops:
  0.6 18.2 %copy-start.1 = (bf16[256,2048]{1,0:T(8,128)(2,1)S(1)}, bf16[256,2048]{1,0:T(8,128)(2,1)}, u32[]{:S(2)}) copy-start(bf16[256,2048]{1,0:T(8,128)(2,1)} %refs_4_.1) | copy-start | bytes 3145732
  0.6 19.6 %copy-start = (bf16[2,7168,64]{1,2,0:T(8,128)(2,1)S(1)}, bf16[2,7168,64]{1,2,0:T(8,128)(2,1)}, u32[]{:S(2)}) copy-start(bf16[2,7168,64]{1,2,0:T(8,128)(2,1)} %param.9) | copy-start | bytes 5505028
  0.7 19.6 %copy-start.3 = (s32[3]{0:T(128)S(1)}, s32[3]{0:T(128)}, u32[]{:S(2)}) copy-start(s32[3]{0:T(128)} %lens_hbm.2) | copy-start | bytes 40
  11.8 34.2 %collective-permute-start.1 = (bf16[128,768]{1,0:T(8,128)(2,1)}, bf16[128,768]{1,0:T(8,128)(2,1)S(1)}, u32[]{:S(2)}, u32[]{:S(2)}) collective-permute-start(bf16[128,768]{1,0:T(8,128)(2,1)} %shard_map.77.refs_0_), channel_id=1, source_target_pairs={{0,4},{4,0},{8,12},{12,8},{1,5},{5,1},{9,13},{13,9},{2,6},{6,2},{1... | collective-permute-start | bytes 589832 | tf_op jit(solution)/shard_map/ppermute | solution.py:303
  13.6 32.4 %collective-permute-start.2 = (bf16[128,768]{1,0:T(8,128)(2,1)}, bf16[128,768]{1,0:T(8,128)(2,1)S(1)}, u32[]{:S(2)}, u32[]{:S(2)}) collective-permute-start(bf16[128,768]{1,0:T(8,128)(2,1)} %shard_map.77.refs_0_), channel_id=1, source_target_pairs={{0,8},{4,12},{8,0},{12,4},{1,9},{5,13},{9,1},{13,5},{2,10},{6,14},... | collective-permute-start | bytes 589832 | tf_op jit(solution)/shard_map/ppermute | solution.py:303
  18.8 27.2 %collective-permute-start.3 = (bf16[128,768]{1,0:T(8,128)(2,1)}, bf16[128,768]{1,0:T(8,128)(2,1)S(1)}, u32[]{:S(2)}, u32[]{:S(2)}) collective-permute-start(bf16[128,768]{1,0:T(8,128)(2,1)} %shard_map.77.refs_0_), channel_id=1, source_target_pairs={{0,12},{4,8},{8,4},{12,0},{1,13},{5,9},{9,5},{13,1},{2,14},{6,10},... | collective-permute-start | bytes 589832 | tf_op jit(solution)/shard_map/ppermute | solution.py:303
  18.8 27.2 %collective-permute-start = (bf16[256,2048]{1,0:T(8,128)(2,1)S(1)}, bf16[256,2048]{1,0:T(8,128)(2,1)S(1)}, u32[]{:S(2)}, u32[]{:S(2)}) collective-permute-start(bf16[256,2048]{1,0:T(8,128)(2,1)S(1)} %copy-done.1), channel_id=1, source_target_pairs={{0,2},{1,3},{2,0},{3,1},{4,6},{5,7},{6,4},{7,5},{8,10},{9,11},{10,... | collective-permute-start | bytes 3145736 | tf_op jit(solution)/shard_map/ppermute | solution.py:303
  20.2 31.2 %collective-permute-start.7 = (bf16[256,2048]{1,0:T(8,128)(2,1)S(1)}, bf16[256,2048]{1,0:T(8,128)(2,1)S(1)}, u32[]{:S(2)}, u32[]{:S(2)}) collective-permute-start(bf16[256,2048]{1,0:T(8,128)(2,1)S(1)} %copy-done.1), channel_id=1, source_target_pairs={{0,1},{1,0},{2,3},{3,2},{4,5},{5,4},{6,7},{7,6},{8,9},{9,8},{10,11... | collective-permute-start | bytes 3145736 | tf_op jit(solution)/shard_map/ppermute | solution.py:303
  20.2 25.9 %copy-start.2 = (bf16[128,768]{1,0:T(8,128)(2,1)S(1)}, bf16[128,768]{1,0:T(8,128)(2,1)}, u32[]{:S(2)}) copy-start(bf16[128,768]{1,0:T(8,128)(2,1)} %shard_map.77.refs_0_) | copy-start | bytes 589828
  46.1 9.6 %collective-permute-start.8 = (bf16[256,2048]{1,0:T(8,128)(2,1)S(1)}, bf16[256,2048]{1,0:T(8,128)(2,1)S(1)}, u32[]{:S(2)}, u32[]{:S(2)}) collective-permute-start(bf16[256,2048]{1,0:T(8,128)(2,1)S(1)} %collective-permute-done.refs_6_), channel_id=1, source_target_pairs={{0,1},{1,0},{2,3},{3,2},{4,5},{5,4},{6,7},{7,6},{8,9},{9,8},{10,11... | collective-permute-start | bytes 3145736 | tf_op jit(solution)/shard_map/ppermute | solution.py:303
  46.9 4.5 %collective-permute-start.4 = (f32[3,16,128]{2,1,0:T(8,128)S(1)}, f32[3,16,128]{2,1,0:T(8,128)S(1)}, u32[]{:S(2)}, u32[]{:S(2)}) collective-permute-start(f32[3,16,128]{2,1,0:T(8,128)S(1)} %get-tuple-element.24), channel_id=1, source_target_pairs={{0,4},{4,0},{8,12},{12,8},{1,5},{5,1},{9,13},{13,9},{2,6},{6,2},{1... | collective-permute-start | bytes 73736 | tf_op jit(solution)/shard_map/ppermute | solution.py:303
  47.5 4.9 %collective-permute-start.5 = (f32[3,16,128]{2,1,0:T(8,128)S(1)}, f32[3,16,128]{2,1,0:T(8,128)S(1)}, u32[]{:S(2)}, u32[]{:S(2)}) collective-permute-start(f32[3,16,128]{2,1,0:T(8,128)S(1)} %get-tuple-element.25), channel_id=1, source_target_pairs={{0,8},{4,12},{8,0},{12,4},{1,9},{5,13},{9,1},{13,5},{2,10},{6,14},... | collective-permute-start | bytes 73736 | tf_op jit(solution)/shard_map/ppermute | solution.py:303
  50.0 5.6 %collective-permute-start.6 = (f32[3,16,128]{2,1,0:T(8,128)S(1)}, f32[3,16,128]{2,1,0:T(8,128)S(1)}, u32[]{:S(2)}, u32[]{:S(2)}) collective-permute-start(f32[3,16,128]{2,1,0:T(8,128)S(1)} %get-tuple-element.26), channel_id=1, source_target_pairs={{0,12},{4,8},{8,4},{12,0},{1,13},{5,9},{9,5},{13,1},{2,14},{6,10},... | collective-permute-start | bytes 73736 | tf_op jit(solution)/shard_map/ppermute | solution.py:303
  57.3 4.6 %collective-permute-start.10 = (f32[3,1024]{1,0:T(4,128)S(1)}, f32[3,1024]{1,0:T(4,128)S(1)}, u32[]{:S(2)}, u32[]{:S(2)}) collective-permute-start(f32[3,1024]{1,0:T(4,128)S(1)} %get-tuple-element.29), channel_id=1, source_target_pairs={{0,8},{4,12},{8,0},{12,4},{1,9},{5,13},{9,1},{13,5},{2,10},{6,14},... | collective-permute-start | bytes 36872 | tf_op jit(solution)/shard_map/ppermute | solution.py:303
  57.3 5.5 %collective-permute-start.11 = (f32[3,1024]{1,0:T(4,128)S(1)}, f32[3,1024]{1,0:T(4,128)S(1)}, u32[]{:S(2)}, u32[]{:S(2)}) collective-permute-start(f32[3,1024]{1,0:T(4,128)S(1)} %get-tuple-element.29), channel_id=1, source_target_pairs={{0,12},{4,8},{8,4},{12,0},{1,13},{5,9},{9,5},{13,1},{2,14},{6,10},... | collective-permute-start | bytes 36872 | tf_op jit(solution)/shard_map/ppermute | solution.py:303
  58.9 4.0 %collective-permute-start.9 = (f32[3,1024]{1,0:T(4,128)S(1)}, f32[3,1024]{1,0:T(4,128)S(1)}, u32[]{:S(2)}, u32[]{:S(2)}) collective-permute-start(f32[3,1024]{1,0:T(4,128)S(1)} %get-tuple-element.29), channel_id=1, source_target_pairs={{0,4},{4,0},{8,12},{12,8},{1,5},{5,1},{9,13},{13,9},{2,6},{6,2},{1... | collective-permute-start | bytes 36872 | tf_op jit(solution)/shard_map/ppermute | solution.py:303
